TPU v7x, 32 devices: a whole 2x2x4 slice. The times are simulated.
32 devices in a mesh: blk: 8 (over z, y), smp: 4 (over x, core).
Axes of the slice: x: 2, y: 2, z: 4, core: 2. Of those that a mesh axis runs over, the one named last changes fastest.
Arguments:
- genotype: bfloat16 [32768, 4096], P('smp', 'blk'), may hold values from -7 to 7
- presence: int32 [6, 4096], P(None, 'blk'), may hold values 0 or 1
- cohort_id: int32 [32768], P('smp'), may hold values from 0 to 5, as said below
- fold_id: int32 [32768], P('smp'), may hold values from 0 to 4
- phenotype: int32 [32768], P('smp'), may hold values from 0 to 1
Outputs:
- level_one: float32 [40], replicated
- linear_pred: float32 [32768], P(('smp', 'blk'))
Inputs may be any that keep to these rules, and one draw needn't show every extreme that they name: Samples are laid out by cohort: cohort_id never falls from one sample to the next.
All inputs are finite; a program needn't handle non-finite values. No bound on the sum of `presence` on one device may be relied on, other than what follows from the above.
Results may differ from a plain program's by a relative error of at most 0.0023.
Values sent between devices are 32-bit elements; how exact they have to be, the bound alone decides.
A program may use at most 128 MiB of HBM per device.

v0:
```python
import jax
import jax.numpy as jnp
from jax import lax
from jax.sharding import PartitionSpec as P

NEWTON = 4
RIDGE_STEPS = 6


penalty_list = (0.002, 0.01, 0.05, 0.25, 1.25)
level_ridge = 0.05


def ridge_solve(gram, cross, shifts, steps):
    high = lax.Precision.HIGHEST
    residual = jnp.broadcast_to(cross[None, :], (shifts.shape[0], cross.shape[0]))
    solution = jnp.zeros_like(residual)
    direction = residual
    norm_now = jnp.sum(residual * residual, axis=1)
    for ridge_step in range(steps):
        image = jnp.dot(direction, gram, precision=high) + shifts[:, None] * direction
        alpha = norm_now / jnp.sum(direction * image, axis=1)
        solution = solution + alpha[:, None] * direction
        residual = residual - alpha[:, None] * image
        norm_next = jnp.sum(residual * residual, axis=1)
        direction = residual + (norm_next / norm_now)[:, None] * direction
        norm_now = norm_next
    return solution


def on_device(genotype, presence, cohort_id, fold_id, phenotype):
    local_count = genotype.shape[0]
    width = genotype.shape[1]
    total_samples = local_count * lax.axis_size("smp")
    train = (fold_id != 0).astype(jnp.float32)
    target = 2.0 * phenotype.astype(jnp.float32) - 1.0
    onehot = (cohort_id[:, None] == jnp.arange(presence.shape[0], dtype=jnp.int32)[None, :]).astype(
        jnp.bfloat16
    )
    present_rows = jnp.dot(
        onehot, presence.astype(jnp.bfloat16), preferred_element_type=jnp.float32
    ).astype(jnp.bfloat16)
    masked = genotype * present_rows
    weighted = masked * train.astype(jnp.bfloat16)[:, None]
    gram = lax.dot_general(
        weighted, masked, (((0,), (0,)), ((), ())), preferred_element_type=jnp.float32
    )
    cross = jnp.dot(
        (train * target).astype(jnp.bfloat16), masked, preferred_element_type=jnp.float32
    )
    gram, cross = lax.psum((gram, cross), "smp")
    shifts = jnp.array([penalty * total_samples for penalty in penalty_list], jnp.float32)
    ridge = ridge_solve(gram, cross, shifts, RIDGE_STEPS).astype(jnp.bfloat16)
    scores = lax.dot_general(
        ridge, masked, (((1,), (1,)), ((), ())), preferred_element_type=jnp.float32
    )
    scores = scores * jnp.sqrt(jnp.float32(total_samples) / width)
    owned = local_count // lax.axis_size("blk")
    offset = lax.axis_index("blk") * owned
    whole = lax.all_gather(scores, "blk", axis=0, tiled=True)
    local_scores = lax.dynamic_slice_in_dim(whole, offset, owned, 1)
    labels = lax.dynamic_slice_in_dim(phenotype.astype(jnp.float32), offset, owned, 0)
    local_train = lax.dynamic_slice_in_dim(train, offset, owned, 0)
    predictors = local_scores.shape[0]
    level_one = jnp.zeros((predictors,), jnp.float32)
    pred_identity = jnp.eye(predictors, dtype=jnp.float32)
    high = lax.Precision.HIGHEST
    for newton_step in range(NEWTON):
        linear = jnp.dot(level_one, local_scores, precision=high)
        prob = jax.nn.sigmoid(linear)
        resid = local_train * (labels - prob)
        curve = local_train * prob * (1.0 - prob)
        grad = jnp.dot(local_scores, resid, precision=high)
        hess = lax.dot_general(
            local_scores * curve[None, :], local_scores, (((1,), (1,)), ((), ())), precision=high
        )
        grad, hess = lax.psum((grad, hess), ("blk", "smp"))
        factor = jnp.linalg.cholesky(hess + level_ridge * total_samples * pred_identity)
        level_one = level_one + jax.scipy.linalg.cho_solve(
            (factor, True), grad - level_ridge * total_samples * level_one
        )
    linear_pred = jnp.dot(level_one, local_scores, precision=high)
    return (level_one, linear_pred)


def solution(mesh):
    in_specs = (P("smp", "blk"), P(None, "blk"), P("smp"), P("smp"), P("smp"))
    out_specs = (P(), P(("smp", "blk")))
    return jax.shard_map(
        on_device, mesh=mesh, in_specs=in_specs, out_specs=out_specs, check_vma=False
    )
```

profile of v0, /device:TPU:0, one launch (start us, length us, event | category | flops | bytes accessed | tf_op | source)
XLA Modules:
  0.0 333.3 jit_solution(6605874779834093445)
XLA Ops:
  7.2 0.8 fusion.102
  8.0 5.8 %fusion.2 = bf16[8192,512]{1,0:T(8,128)(2,1)S(1)} fusion(bf16[8192,512]{1,0:T(8,128)(2,1)} %param.9, s32[8192]{0:T(1024)} %param.11, s32[6,512]{1,0:T(8,128)} %param.10), kind=kOutput, calls=%fused_computation.3 | convolution fusion | flops 58772480 | bytes 16822272 | tf_op jit(solution)/shard_map/dot_general | solution.py:40
  13.8 3.2 copy-done
  17.0 5.9 %fusion = f32[512,512]{1,0:T(8,128)} fusion(bf16[8192,512]{1,0:T(8,128)(2,1)S(1)} %fusion.2, bf16[8192]{0:T(1024)(128)(2,1)S(1)} %convert_convert_fusion), kind=kOutput, calls=%fused_computation | convolution fusion | flops 4299161600 | bytes 9453568 | tf_op jit(solution)/shard_map/dot_general | solution.py:45
  23.0 4.6 %fusion.103 = f32[1,512]{1,0:T(1,128)S(1)} fusion(bf16[8192,1]{0,1:T(2,128)(2,1)S(1)} %reshape.82, bf16[8192,512]{1,0:T(8,128)(2,1)} %copy-done), kind=kOutput, calls=%fused_computation.185 | convolution fusion | flops 8388608 | bytes 8407040 | tf_op jit(solution)/shard_map/dot_general | solution.py:48
  27.6 8.7 %psum.70 = f32[512]{0:T(512)S(1)} all-reduce(f32[512]{0:T(512)S(1)} %bitcast.149), channel_id=1, replica_groups=mesh['blk'=8,'smp'=4] {'smp'}, use_global_device_ids=true, to_apply=%region_0.0 | all-reduce | flops 512 | bytes 4096 | tf_op jit(solution)/shard_map/psum | solution.py:51
  36.9 25.0 %all-reduce.6.cloned.1.call-done = f32[512,512]{1,0:T(8,128)} async-done(((f32[512,512]{1,0:T(8,128)}), f32[512,512]{1,0:T(8,128)}) %all-reduce.6.cloned.1.call-update) | async-done | bytes 1048592 | tf_op jit(solution)/shard_map/psum | solution.py:51
  61.9 2.0 multiply_reduce_fusion.9
  70.2 6.4 %fusion.3 = f32[1,5,8192]{2,1,0:T(8,128)} fusion(bf16[8192,512]{1,0:T(8,128)(2,1)} %copy-done, f32[5,512]{1,0:T(8,128)S(1)} %multiply_add_fusion.1, f32[5,512]{1,0:T(8,128)S(1)} %multiply_add_fusion.2, f32[5,512]{1,0:T(8,128)S(1)} %multiply_add_fusion.3, f32[5]{0:T(128)S(1)} %div.105, f32[5,512]{1,0:T(8,128)S(1)} %get-tuple-element.15, f32[5]{0:T(128)S(1)} %div.104, ...), kind=kOutput, calls=%fused_computation.5 | convolution fusion | flops 42030080 | bytes 8605856 | tf_op jit(solution)/shard_map/dot_general | solution.py:54
  76.6 49.8 %all-gather.3.cloned.1.call-done = f32[8,5,8192]{2,1,0:T(8,128)} async-done(((f32[1,5,8192]{2,1,0:T(8,128)}), f32[8,5,8192]{2,1,0:T(8,128)}) %all-gather.3.cloned.1.call-update) | async-done | bytes 1310736 | tf_op jit(solution)/shard_map/all_gather | solution.py:60
  126.4 1.8 reshape.81
  129.0 39.5 %all-reduce.3 = (f32[40,40]{0,1:T(8,128)S(1)}, f32[40]{0:T(128)S(1)}) all-reduce(f32[40,40]{0,1:T(8,128)S(1)} %fusion.16, f32[40]{0:T(128)S(1)} %convolution_bitcast_fusion.10), channel_id=1, replica_groups=mesh['blk'=8,'smp'=4] {'blk','smp'}, use_global_device_ids=true, to_apply=%region_14.0 | all-reduce | flops 1640 | bytes 13120 | tf_op jit(solution)/shard_map/psum | solution.py:77
  168.6 3.6 %cholesky.74 = f32[40,40]{1,0:T(8,128)S(1)} custom-call(f32[40,40]{1,0:T(8,128)S(1)} %fusion.57), custom_call_target="Cholesky" | custom-call | tf_op jit(solution)/shard_map/jit(cholesky)/cholesky | solution.py:78
  173.6 3.1 custom-call.10
  177.8 40.2 %all-reduce.2 = (f32[40,40]{0,1:T(8,128)S(1)}, f32[40]{0:T(128)S(1)}) all-reduce(f32[40,40]{0,1:T(8,128)S(1)} %fusion.14, f32[40]{0:T(128)S(1)} %convolution_bitcast_fusion.9), channel_id=1, replica_groups=mesh['blk'=8,'smp'=4] {'blk','smp'}, use_global_device_ids=true, to_apply=%region_18.0 | all-reduce | flops 1640 | bytes 13120 | tf_op jit(solution)/shard_map/psum | solution.py:77
  218.1 3.6 %cholesky.85 = f32[40,40]{1,0:T(8,128)S(1)} custom-call(f32[40,40]{1,0:T(8,128)S(1)} %fusion.53), custom_call_target="Cholesky" | custom-call | tf_op jit(solution)/shard_map/jit(cholesky)/cholesky | solution.py:78
  223.0 3.1 custom-call.11
  227.2 40.6 %all-reduce.1 = (f32[40,40]{0,1:T(8,128)S(1)}, f32[40]{0:T(128)S(1)}) all-reduce(f32[40,40]{0,1:T(8,128)S(1)} %fusion.12, f32[40]{0:T(128)S(1)} %convolution_bitcast_fusion.8), channel_id=1, replica_groups=mesh['blk'=8,'smp'=4] {'blk','smp'}, use_global_device_ids=true, to_apply=%region_20.0 | all-reduce | flops 1640 | bytes 13120 | tf_op jit(solution)/shard_map/psum | solution.py:77
  267.9 3.6 %cholesky.96 = f32[40,40]{1,0:T(8,128)S(1)} custom-call(f32[40,40]{1,0:T(8,128)S(1)} %fusion.50), custom_call_target="Cholesky" | custom-call | tf_op jit(solution)/shard_map/jit(cholesky)/cholesky | solution.py:78
  272.9 3.1 custom-call.12
  277.0 40.2 %all-reduce = (f32[40,40]{0,1:T(8,128)S(1)}, f32[40]{0:T(128)S(1)}) all-reduce(f32[40,40]{0,1:T(8,128)S(1)} %fusion.10, f32[40]{0:T(128)S(1)} %convolution_bitcast_fusion.7), channel_id=1, replica_groups=mesh['blk'=8,'smp'=4] {'blk','smp'}, use_global_device_ids=true, to_apply=%region_22.25 | all-reduce | flops 1640 | bytes 13120 | tf_op jit(solution)/shard_map/psum | solution.py:77
  317.3 3.6 %cholesky.107 = f32[40,40]{1,0:T(8,128)S(1)} custom-call(f32[40,40]{1,0:T(8,128)S(1)} %fusion.47), custom_call_target="Cholesky" | custom-call | tf_op jit(solution)/shard_map/jit(cholesky)/cholesky | solution.py:78
  322.3 3.1 custom-call.13
  325.6 0.8 fusion.37
  (90 shorter events, 16.9 us)
Async XLA Ops:
  7.2 54.7 %all-reduce.6.cloned.1.call-start = ((), (), s32[]{:S(2)}) async-start(), calls=%async_computation | async-start | bytes 2097152 | tf_op jit(solution)/shard_map/psum | solution.py:51
  13.8 3.2 copy-start
  17.0 6.0 %copy-start.2 = (s32[8192]{0:T(1024)S(1)}, s32[8192]{0:T(1024)}, u32[]{:S(2)}) copy-start(s32[8192]{0:T(1024)} %param.13) | copy-start | bytes 98308
  22.9 103.5 %all-gather.3.cloned.1.call-start = ((), (), s32[]{:S(2)}) async-start(), calls=%async_computation.1 | async-start | bytes 2359296 | tf_op jit(solution)/shard_map/all_gather | solution.py:60
  23.0 38.8 %copy-start.3 = (f32[5]{0:T(128)S(1)}, f32[5]{0:T(128)}, u32[]{:S(2)}) copy-start(f32[5]{0:T(128)} %constant.67.clone) | copy-start | bytes 64
  61.9 3.5 %copy-start.1 = (f32[512,512]{1,0:T(8,128)S(1)}, f32[512,512]{1,0:T(8,128)}, u32[]{:S(2)}) copy-start(f32[512,512]{1,0:T(8,128)} %all-reduce.6.cloned.1.call-done) | copy-start | bytes 3145732
  325.6 0.8 copy-start.4
Sparse Core Ops, SparseCore 0:
  23.1 38.7 all-reduce.5
  76.7 49.6 all-gather.2
where the time goes:
time: 334 us; the launch traced here: 333 us
  blocking collectives  169 us (51%)
  waiting for transfers between devices  74.8 us (22%)
  other arithmetic  36.2 us (11%)
  matrix products  33.4 us (10%)
  between operations  14.3 us (4%)
  local copies, waits for them, and re-layouts  5.38 us (2%)
    psum x4, blocking collectives, on_device(): grad, hess = lax.psum((grad, hess), ('blk', 'smp'))  160 us
    all_gather x1, waiting for transfers between devices, on_device(): whole = lax.all_gather(scores, 'blk', axis=0, tiled=True)  49.8 us
    psum x1, waiting for transfers between devices, on_device(): gram, cross = lax.psum((gram, cross), 'smp')  25 us
    another operation x12, other arithmetic, on_device(): jnp.linalg.cholesky(hess + level_ridge * total_samples * pred_identity)  17.3 us
    another operation x8, other arithmetic, on_device(): jax.scipy.linalg.cho_solve((factor, True), grad - level_ridge * total_sam...  14.8 us
    psum x1, blocking collectives, on_device(): gram, cross = lax.psum((gram, cross), 'smp')  8.68 us
  transfers between devices with their start and end apart: 2, of which 2 were waited for; matrix products, arithmetic and copies ran while one was open for 2% of the time, Pallas kernels for 0%

commit v1 on v0

--- a/solution.py
+++ b/solution.py
@@ -1,10 +1,17 @@
+import functools
+
 import jax
 import jax.numpy as jnp
 from jax import lax
+from jax.experimental import pallas as pl
+from jax.experimental.pallas import tpu as pltpu
 from jax.sharding import PartitionSpec as P
 
 NEWTON = 4
 RIDGE_STEPS = 6
+PANEL = 8
+LANES = 128
+MESH = pl.DeviceIdType.MESH
 
 
 penalty_list = (0.002, 0.01, 0.05, 0.25, 1.25)
@@ -28,6 +35,185 @@
     return solution
 
 
+def low_part(value):
+    return value - value.astype(jnp.bfloat16).astype(jnp.float32)
+
+
+def spd_solve(system, order):
+    width = system.shape[1]
+    row_of = lax.broadcasted_iota(jnp.int32, (order, width), 0)
+    row_of_lane = lax.broadcasted_iota(jnp.int32, (order, LANES), 0)
+    for start in range(0, order, PANEL):
+        stop = min(start + PANEL, order)
+        columns = [
+            jnp.broadcast_to(system[:, j : j + 1], (order, LANES)) for j in range(start, stop)
+        ]
+        for j in range(start, stop):
+            column = columns[j - start]
+            inverse = 1.0 / column[j : j + 1, :]
+            pivot_row = system[j : j + 1, :] * jnp.concatenate(
+                [inverse] * pl.cdiv(width, LANES), axis=1
+            )[:, :width]
+            wide = jnp.concatenate([column] * pl.cdiv(width, LANES), axis=1)[:, :width]
+            system = jnp.where(row_of == j, pivot_row, system - wide * pivot_row)
+            for k in range(j + 1, stop):
+                other = columns[k - start]
+                entry = other[j : j + 1, :] * inverse
+                columns[k - start] = jnp.where(row_of_lane == j, entry, other - column * entry)
+    return jnp.broadcast_to(system[:, order : order + 1], (order, LANES))
+
+
+def exchange(ref, mine, axis, count, send_sem, recv_sem):
+    copies = []
+    for distance in range(1, count):
+        copy = pltpu.make_async_remote_copy(
+            src_ref=ref.at[mine],
+            dst_ref=ref.at[mine],
+            send_sem=send_sem.at[distance],
+            recv_sem=recv_sem.at[distance],
+            device_id={axis: lax.rem(mine + distance, count)},
+            device_id_type=MESH,
+        )
+        copy.start()
+        copies.append(copy)
+    for copy in copies:
+        copy.wait_recv()
+    total = ref[0]
+    for slot in range(1, count):
+        total = total + ref[slot]
+    for copy in copies:
+        copy.wait_send()
+    return total
+
+
+def level_one_kernel(
+    blk, smp, total_samples,
+    scores_ref, fold_ref, pheno_ref, level_ref, linear_ref,
+    gathered, packed, pieces, smp_part, blk_part,
+    score_send, score_recv, smp_send, smp_recv, blk_send, blk_recv,
+):
+    mine_b = lax.axis_index("blk")
+    mine_s = lax.axis_index("smp")
+    per_block = scores_ref.shape[0]
+    owned = packed.shape[1]
+    predictors = packed.shape[0]
+    barrier = pltpu.get_barrier_semaphore()
+    for distance in range(1, blk):
+        pl.semaphore_signal(
+            barrier, inc=1, device_id={"blk": lax.rem(mine_b + distance, blk)}, device_id_type=MESH
+        )
+    for distance in range(1, smp):
+        pl.semaphore_signal(
+            barrier, inc=1, device_id={"smp": lax.rem(mine_s + distance, smp)}, device_id_type=MESH
+        )
+    pl.semaphore_wait(barrier, blk + smp - 2)
+
+    copies = []
+    for distance in range(1, blk):
+        target = lax.rem(mine_b + distance, blk)
+        copy = pltpu.make_async_remote_copy(
+            src_ref=scores_ref.at[:, pl.ds(pl.multiple_of(target * owned, LANES), owned)],
+            dst_ref=gathered.at[mine_b],
+            send_sem=score_send.at[distance],
+            recv_sem=score_recv.at[distance],
+            device_id={"blk": target},
+            device_id_type=MESH,
+        )
+        copy.start()
+        copies.append(copy)
+    own = pl.ds(pl.multiple_of(mine_b * owned, LANES), owned)
+    gathered[mine_b] = scores_ref[:, own]
+    labels = pheno_ref[:, own].astype(jnp.float32)
+    train = (fold_ref[:, own] != 0).astype(jnp.float32)
+    for copy in copies:
+        copy.wait_recv()
+    for block in range(blk):
+        packed[block * per_block : (block + 1) * per_block, :] = gathered[block]
+    scores = packed[...]
+    pieces[...] = jnp.concatenate([scores, low_part(scores)], axis=0).astype(jnp.bfloat16)
+    for copy in copies:
+        copy.wait_send()
+
+    width = predictors + 8
+    pad_row = lax.broadcasted_iota(jnp.int32, (8, owned), 0)
+    row_of = lax.broadcasted_iota(jnp.int32, (predictors, width), 0)
+    column_of = lax.broadcasted_iota(jnp.int32, (predictors, width), 1)
+    ridge = level_ridge * total_samples
+
+    def predict(level):
+        return jnp.sum(
+            packed[...] * jnp.concatenate([level] * (owned // LANES), axis=1), axis=0, keepdims=True
+        )
+
+    def widen(level):
+        return jnp.concatenate([level] * pl.cdiv(width, LANES), axis=1)[:, :width]
+
+    def newton(step, level):
+        prob = jax.nn.sigmoid(predict(level))
+        resid = train * (labels - prob)
+        curve = train * prob * (1.0 - prob)
+        right = jnp.concatenate(
+            [packed[...] * curve, jnp.where(pad_row == 0, resid, 0.0)], axis=0
+        )
+        moments = jnp.zeros((2 * predictors, width), jnp.float32)
+        for part in (right, low_part(right)):
+            moments = moments + lax.dot_general(
+                pieces[...], part.astype(jnp.bfloat16), (((1,), (1,)), ((), ())),
+                preferred_element_type=jnp.float32,
+            )
+        smp_part[step, mine_s] = moments[:predictors] + moments[predictors:]
+        over_smp = exchange(
+            smp_part.at[step], mine_s, "smp", smp, smp_send.at[step], smp_recv.at[step]
+        )
+        blk_part[step, mine_b] = over_smp
+        system = exchange(
+            blk_part.at[step], mine_b, "blk", blk, blk_send.at[step], blk_recv.at[step]
+        )
+        system = jnp.where(row_of == column_of, system + ridge, system)
+        system = jnp.where(column_of == predictors, system - ridge * widen(level), system)
+        return level + spd_solve(system, predictors)
+
+    level = lax.fori_loop(0, NEWTON, newton, jnp.zeros((predictors, LANES), jnp.float32))
+    linear_ref[...] = predict(level)
+    diagonal = row_of == column_of
+    level_ref[...] = jnp.sum(jnp.where(diagonal, widen(level), 0.0), axis=0, keepdims=True)[
+        :, :predictors
+    ]
+
+
+def level_one_fit(scores, fold_id, phenotype, total_samples):
+    blk = lax.axis_size("blk")
+    smp = lax.axis_size("smp")
+    per_block, local_count = scores.shape
+    owned = local_count // blk
+    predictors = per_block * blk
+    width = predictors + 8
+    dma = pltpu.SemaphoreType.DMA
+    level, linear = pl.pallas_call(
+        functools.partial(level_one_kernel, blk, smp, total_samples),
+        out_shape=(
+            jax.ShapeDtypeStruct((1, predictors), jnp.float32),
+            jax.ShapeDtypeStruct((1, owned), jnp.float32),
+        ),
+        in_specs=[pl.BlockSpec(memory_space=pltpu.VMEM)] * 3,
+        out_specs=(pl.BlockSpec(memory_space=pltpu.VMEM),) * 2,
+        scratch_shapes=[
+            pltpu.VMEM((blk, per_block, owned), jnp.float32),
+            pltpu.VMEM((predictors, owned), jnp.float32),
+            pltpu.VMEM((2 * predictors, owned), jnp.bfloat16),
+            pltpu.VMEM((NEWTON, smp, predictors, width), jnp.float32),
+            pltpu.VMEM((NEWTON, blk, predictors, width), jnp.float32),
+            dma((blk,)), dma((blk,)),
+            dma((NEWTON, smp)), dma((NEWTON, smp)),
+            dma((NEWTON, blk)), dma((NEWTON, blk)),
+        ],
+        compiler_params=pltpu.CompilerParams(
+            collective_id=0, has_side_effects=True, vmem_limit_bytes=48 * 1024 * 1024
+        ),
+    )(scores, fold_id.reshape(1, -1), phenotype.reshape(1, -1))
+    return level.reshape(predictors), linear.reshape(owned)
+
+
 def on_device(genotype, presence, cohort_id, fold_id, phenotype):
     local_count = genotype.shape[0]
     width = genotype.shape[1]
@@ -55,32 +241,7 @@
         ridge, masked, (((1,), (1,)), ((), ())), preferred_element_type=jnp.float32
     )
     scores = scores * jnp.sqrt(jnp.float32(total_samples) / width)
-    owned = local_count // lax.axis_size("blk")
-    offset = lax.axis_index("blk") * owned
-    whole = lax.all_gather(scores, "blk", axis=0, tiled=True)
-    local_scores = lax.dynamic_slice_in_dim(whole, offset, owned, 1)
-    labels = lax.dynamic_slice_in_dim(phenotype.astype(jnp.float32), offset, owned, 0)
-    local_train = lax.dynamic_slice_in_dim(train, offset, owned, 0)
-    predictors = local_scores.shape[0]
-    level_one = jnp.zeros((predictors,), jnp.float32)
-    pred_identity = jnp.eye(predictors, dtype=jnp.float32)
-    high = lax.Precision.HIGHEST
-    for newton_step in range(NEWTON):
-        linear = jnp.dot(level_one, local_scores, precision=high)
-        prob = jax.nn.sigmoid(linear)
-        resid = local_train * (labels - prob)
-        curve = local_train * prob * (1.0 - prob)
-        grad = jnp.dot(local_scores, resid, precision=high)
-        hess = lax.dot_general(
-            local_scores * curve[None, :], local_scores, (((1,), (1,)), ((), ())), precision=high
-        )
-        grad, hess = lax.psum((grad, hess), ("blk", "smp"))
-        factor = jnp.linalg.cholesky(hess + level_ridge * total_samples * pred_identity)
-        level_one = level_one + jax.scipy.linalg.cho_solve(
-            (factor, True), grad - level_ridge * total_samples * level_one
-        )
-    linear_pred = jnp.dot(level_one, local_scores, precision=high)
-    return (level_one, linear_pred)
+    return level_one_fit(scores, fold_id, phenotype, total_samples)
 
 
 def solution(mesh):

time: 334 us -> 141 us (0.42)
  blocking collectives: 169 us -> 8.68 us
  Pallas kernels: 0 us -> 50.3 us
  waiting for transfers between devices: 74.8 us -> 25.3 us
  other arithmetic: 36.2 us -> 3.93 us
    psum x4 -> x0, blocking collectives: 160 us -> none  [on_device(): grad, hess = lax.psum((grad, hess), ('blk', 'smp'))]
    pallas_call x0 -> x1, Pallas kernels: none -> 50.3 us  [level_one_fit(): pl.pallas_call(functools.partial(level_one_kernel, blk, smp, total_sample...]
    all_gather x1 -> x0, waiting for transfers between devices: 49.8 us -> none  [on_device(): whole = lax.all_gather(scores, 'blk', axis=0, tiled=True)]
    another operation x20 -> x0, other arithmetic: 32.1 us -> none  [the longest x12 17.3 us: on_device(): jnp.linalg.cholesky(hess + level_ridge * total_samples * pred_identity)]
    dot_general x6, matrix products: 5.68 us -> 11.7 us  [ridge_solve(): jnp.dot(direction, gram, precision=high) + shifts[:, None] * direction]
    dot_general x13 -> x0, matrix products: 3.83 us -> none  [the longest x4 1.3 us: on_device(): lax.dot_general(local_scores * curve[None, :], local_scores, (((1,), (1,)...]
  transfers between devices with their start and end apart: 2 -> 1, of which waited for: 2 -> 1; matrix products, arithmetic and copies ran while one was open for 2% -> 4% of each run, Pallas kernels for 0% -> 0%
where the time goes in v1:
time: 141 us; the launch traced here: 140 us
  Pallas kernels  50.3 us (36%)
  matrix products  33.6 us (24%)
  waiting for transfers between devices  25.3 us (18%)
  between operations  14.1 us (10%)
  blocking collectives  8.68 us (6%)
  local copies, waits for them, and re-layouts  4.35 us (3%)
  other arithmetic  3.93 us (3%)
    pallas_call x1, Pallas kernels, level_one_fit(): pl.pallas_call(functools.partial(level_one_kernel, blk, smp, total_sample...  50.3 us
    psum x1, waiting for transfers between devices, on_device(): gram, cross = lax.psum((gram, cross), 'smp')  25.3 us
    dot_general x6, matrix products, ridge_solve(): jnp.dot(direction, gram, precision=high) + shifts[:, None] * direction  11.7 us
    psum x1, blocking collectives, on_device(): gram, cross = lax.psum((gram, cross), 'smp')  8.68 us
    dot_general x1, matrix products, on_device(): lax.dot_general(weighted, masked, (((0,), (0,)), ((), ())), preferred_ele...  5.86 us
    dot_general x1, matrix products, on_device(): jnp.dot(onehot, presence.astype(jnp.bfloat16), preferred_element_type=jnp...  5.82 us
    dot_general x1, matrix products, on_device(): lax.dot_general(ridge, masked, (((1,), (1,)), ((), ())), preferred_elemen...  5.66 us
    dot_general x1, matrix products, on_device(): jnp.dot((train * target).astype(jnp.bfloat16), masked, preferred_element_...  4.56 us
  transfers between devices with their start and end apart: 1, of which 1 were waited for; matrix products, arithmetic and copies ran while one was open for 4% of the time, Pallas kernels for 0%

profile of v1, /device:TPU:0, one launch (start us, length us, event | category | flops | bytes accessed | tf_op | source)
XLA Modules:
  0.0 140.4 jit_solution(13077874002930178943)
XLA Ops:
  7.2 0.8 select_convert_fusion
  8.0 5.8 %fusion.2 = bf16[8192,512]{1,0:T(8,128)(2,1)S(1)} fusion(bf16[8192,512]{1,0:T(8,128)(2,1)} %param.6, s32[8192]{0:T(1024)} %param.8, s32[6,512]{1,0:T(8,128)} %param.7), kind=kOutput, calls=%fused_computation.3 | convolution fusion | flops 58772480 | bytes 16822272 | tf_op jit(solution)/shard_map/dot_general | solution.py:226
  13.8 3.2 %copy-done.2 = bf16[8192,512]{1,0:T(8,128)(2,1)} copy-done((bf16[8192,512]{1,0:T(8,128)(2,1)}, bf16[8192,512]{1,0:T(8,128)(2,1)S(1)}, u32[]{:S(2)}) %copy-start.2) | copy-done | bytes 8388632
  17.1 5.9 %fusion = f32[512,512]{1,0:T(8,128)} fusion(bf16[8192,512]{1,0:T(8,128)(2,1)S(1)} %fusion.2, bf16[8192]{0:T(1024)(128)(2,1)S(1)} %convert_convert_fusion), kind=kOutput, calls=%fused_computation | convolution fusion | flops 4299161600 | bytes 9453568 | tf_op jit(solution)/shard_map/dot_general | solution.py:231
  23.0 4.6 %fusion.16 = f32[1,512]{1,0:T(1,128)S(1)} fusion(bf16[8192,1]{0,1:T(2,128)(2,1)S(1)} %reshape.75, bf16[8192,512]{1,0:T(8,128)(2,1)} %copy-done.2), kind=kOutput, calls=%fused_computation.52 | convolution fusion | flops 8388608 | bytes 8407040 | tf_op jit(solution)/shard_map/dot_general | solution.py:234
  27.5 8.7 %psum.14 = f32[512]{0:T(512)S(1)} all-reduce(f32[512]{0:T(512)S(1)} %bitcast.22), channel_id=1, replica_groups=mesh['blk'=8,'smp'=4] {'smp'}, use_global_device_ids=true, to_apply=%region_0.0 | all-reduce | flops 512 | bytes 4096 | tf_op jit(solution)/shard_map/psum | solution.py:237
  36.2 0.6 multiply_reduce_fusion.10
  36.8 25.3 %all-reduce.2.cloned.1.call-done = f32[512,512]{1,0:T(8,128)} async-done(((f32[512,512]{1,0:T(8,128)}), f32[512,512]{1,0:T(8,128)}) %all-reduce.2.cloned.1.call-update) | async-done | bytes 1048592 | tf_op jit(solution)/shard_map/psum | solution.py:237
  62.1 1.9 %multiply_reduce_fusion.9 = (f32[5]{0:T(128)S(1)}, f32[5,512]{1,0:T(8,128)S(1)}) fusion(f32[512]{0:T(512)S(1)} %psum.14, f32[5]{0:T(128)S(1)} %copy-done.3, f32[512,512]{1,0:T(8,128)} %all-reduce.2.cloned.1.call-done), kind=kOutput, calls=%fused_computation.38 | convolution fusion | flops 15738875 | bytes 1060904 | tf_op jit(solution)/shard_map/dot_general | solution.py:28
  64.0 0.7 broadcast_divide_fusion.1
  64.9 0.7 broadcast_divide_fusion
  65.5 2.0 %multiply_reduce_fusion.7 = (f32[5]{0:T(128)S(1)}, f32[5,512]{1,0:T(8,128)S(1)}) fusion(f32[5]{0:T(128)S(1)} %broadcast_divide_fusion, f32[5,512]{1,0:T(8,128)S(1)} %get-tuple-element.17, f32[5]{0:T(128)S(1)} %broadcast_divide_fusion.1, f32[512]{0:T(512)S(1)} %psum.14, f32[5]{0:T(128)S(1)} %copy-done.3, f32[512,512]{1,0:T(8,128)} %all-reduce.2.cloned.1.call-done), kind=kOutput, calls=%fused_computation.34 | convolution fusion | flops 15759355 | bytes 1071184 | tf_op jit(solution)/shard_map/dot_general | solution.py:28
  67.5 0.2 multiply_reduce_fusion.6
  67.8 2.0 %multiply_reduce_fusion.5 = (f32[5]{0:T(128)S(1)}, f32[5,512]{1,0:T(8,128)S(1)}) fusion(f32[5,512]{1,0:T(8,128)S(1)} %multiply_add_fusion.3, f32[5]{0:T(128)S(1)} %copy-done.3, f32[512,512]{1,0:T(8,128)} %all-reduce.2.cloned.1.call-done), kind=kOutput, calls=%fused_computation.30 | convolution fusion | flops 15738875 | bytes 1069096 | tf_op jit(solution)/shard_map/dot_general | solution.py:28
  69.8 0.2 multiply_reduce_fusion.4
  70.1 2.0 %multiply_reduce_fusion.3 = (f32[5]{0:T(128)S(1)}, f32[5,512]{1,0:T(8,128)S(1)}) fusion(f32[5,512]{1,0:T(8,128)S(1)} %multiply_add_fusion.2, f32[5]{0:T(128)S(1)} %copy-done.3, f32[512,512]{1,0:T(8,128)} %all-reduce.2.cloned.1.call-done), kind=kOutput, calls=%fused_computation.26 | convolution fusion | flops 15738875 | bytes 1069096 | tf_op jit(solution)/shard_map/dot_general | solution.py:28
  72.0 0.2 multiply_reduce_fusion.2
  72.3 2.0 %multiply_reduce_fusion.1 = (f32[5]{0:T(128)S(1)}, f32[5,512]{1,0:T(8,128)S(1)}) fusion(f32[5,512]{1,0:T(8,128)S(1)} %multiply_add_fusion.1, f32[5]{0:T(128)S(1)} %copy-done.3, f32[512,512]{1,0:T(8,128)} %all-reduce.2.cloned.1.call-done), kind=kOutput, calls=%fused_computation.22 | convolution fusion | flops 15738875 | bytes 1069096 | tf_op jit(solution)/shard_map/dot_general | solution.py:28
  74.3 0.2 multiply_reduce_fusion
  74.5 2.0 %fusion.5 = f32[5]{0:T(128)S(1)} fusion(f32[512,512]{1,0:T(8,128)} %all-reduce.2.cloned.1.call-done, f32[5,512]{1,0:T(8,128)S(1)} %get-tuple-element.7, f32[5,512]{1,0:T(8,128)S(1)} %multiply_add_fusion.1, f32[5]{0:T(128)S(1)} %div.86, f32[5]{0:T(128)S(1)} %copy-done.3), kind=kOutput, calls=%fused_computation.13 | convolution fusion | flops 15749115 | bytes 1069116 | tf_op jit(solution)/shard_map/dot_general | solution.py:28
  76.4 5.7 %convolution_multiply_fusion.scores_ref = f32[5,8192]{1,0:T(8,128)S(1)} fusion(bf16[8192,512]{1,0:T(8,128)(2,1)} %copy-done.2, f32[5,512]{1,0:T(8,128)S(1)} %multiply_add_fusion.1, f32[5,512]{1,0:T(8,128)S(1)} %multiply_add_fusion.2, f32[5,512]{1,0:T(8,128)S(1)} %multiply_add_fusion.3, f32[5]{0:T(128)S(1)} %div.87, f32[5,512]{1,0:T(8,128)S(1)} %get-tuple-element.7, ...), kind=kOutput, calls=%fused_computation.4 | convolution fusion | flops 42030080 | bytes 8605856 | tf_op jit(solution)/shard_map/dot_general | solution.py:240
  82.1 50.3 %shard_map.77 = (f32[1,40]{1,0:T(1,128)S(1)}, f32[1,1024]{1,0:T(1,128)S(1)}) custom-call(f32[5,8192]{1,0:T(8,128)S(1)} %convolution_multiply_fusion.scores_ref, s32[1,8192]{1,0:T(1,128)S(1)} %bitcast.19, s32[1,8192]{1,0:T(1,128)S(1)} %bitcast.18), custom_call_target="tpu_custom_call" | custom-call | tf_op jit(solution)/shard_map/pallas_call | solution.py:192
  132.4 0.5 copy.11
  132.9 0.6 copy.12
  (24 shorter events, 0.6 us)
Async XLA Ops:
  7.2 54.9 %all-reduce.2.cloned.1.call-start = ((), (), s32[]{:S(2)}) async-start(), calls=%async_computation | async-start | bytes 2097152 | tf_op jit(solution)/shard_map/psum | solution.py:237
  13.8 3.2 %copy-start.2 = (bf16[8192,512]{1,0:T(8,128)(2,1)}, bf16[8192,512]{1,0:T(8,128)(2,1)S(1)}, u32[]{:S(2)}) copy-start(bf16[8192,512]{1,0:T(8,128)(2,1)S(1)} %fusion.2) | copy-start | bytes 25165828
  22.9 39.2 %copy-start.3 = (f32[5]{0:T(128)S(1)}, f32[5]{0:T(128)}, u32[]{:S(2)}) copy-start(f32[5]{0:T(128)} %constant.14.clone) | copy-start | bytes 64
  69.7 12.3 %copy-start = (s32[8192]{0:T(1024)S(1)}, s32[8192]{0:T(1024)}, u32[]{:S(2)}) copy-start(s32[8192]{0:T(1024)} %param.10) | copy-start | bytes 98308
  69.8 12.3 %copy-start.1 = (s32[8192]{0:T(1024)S(1)}, s32[8192]{0:T(1024)}, u32[]{:S(2)}) copy-start(s32[8192]{0:T(1024)} %param.9) | copy-start | bytes 98308
Sparse Core Ops, SparseCore 0:
  23.1 38.9 all-reduce.1

commit v2 on v1

--- a/solution.py
+++ b/solution.py
@@ -11,28 +11,14 @@
 RIDGE_STEPS = 6
 PANEL = 8
 LANES = 128
+TILE = 256
+PARTS = 7
+CHUNK = 1024
 MESH = pl.DeviceIdType.MESH
 
 
 penalty_list = (0.002, 0.01, 0.05, 0.25, 1.25)
 level_ridge = 0.05
-
-
-def ridge_solve(gram, cross, shifts, steps):
-    high = lax.Precision.HIGHEST
-    residual = jnp.broadcast_to(cross[None, :], (shifts.shape[0], cross.shape[0]))
-    solution = jnp.zeros_like(residual)
-    direction = residual
-    norm_now = jnp.sum(residual * residual, axis=1)
-    for ridge_step in range(steps):
-        image = jnp.dot(direction, gram, precision=high) + shifts[:, None] * direction
-        alpha = norm_now / jnp.sum(direction * image, axis=1)
-        solution = solution + alpha[:, None] * direction
-        residual = residual - alpha[:, None] * image
-        norm_next = jnp.sum(residual * residual, axis=1)
-        direction = residual + (norm_next / norm_now)[:, None] * direction
-        norm_now = norm_next
-    return solution
 
 
 def low_part(value):
@@ -86,10 +72,165 @@
     return total
 
 
-def level_one_kernel(
-    blk, smp, total_samples,
-    scores_ref, fold_ref, pheno_ref, level_ref, linear_ref,
+def gram_rows(width):
+    return sum(stop + 8 for stop in range(TILE, width + 1, TILE))
+
+
+def accumulate_gram(chunk, chunks, load, geno, pres, cohort_ref, fold_ref, pheno_ref, gram):
+    width = geno.shape[1]
+    cohorts = lax.broadcasted_iota(jnp.int32, (pres.shape[0], chunk), 0)
+    gram[...] = jnp.zeros_like(gram)
+
+    def body(index, _):
+        load(index).wait()
+        rows = pl.ds(pl.multiple_of(index * chunk, chunk), chunk)
+        train = fold_ref[:, rows] != 0
+        member = jnp.where((cohort_ref[:, rows] == cohorts) & train, 1.0, 0.0).astype(jnp.bfloat16)
+        present = lax.dot_general(
+            member, pres[...].astype(jnp.bfloat16), (((0,), (0,)), ((), ())),
+            preferred_element_type=jnp.float32,
+        )
+        weighted = geno[rows, :] * present.astype(jnp.bfloat16)
+        target = 2.0 * pheno_ref[:, rows].astype(jnp.float32) - 1.0
+        target = jnp.broadcast_to(target, (16, chunk)).astype(jnp.bfloat16)
+        flipped = weighted.T
+        start = 0
+        for stop in range(TILE, width + 1, TILE):
+            left = jnp.concatenate([flipped[:stop], target], axis=0)
+            part = jnp.dot(
+                left, weighted[:, stop - TILE : stop], preferred_element_type=jnp.float32
+            )
+            gram[start : start + stop + 8, :] += part[: stop + 8]
+            start += stop + 8
+        return 0
+
+    lax.fori_loop(0, chunks, body, 0)
+
+
+def sum_gram(gram, from_core, over_chip, mine_s, smp, sems):
+    core_send, core_recv, chip_send, chip_recv, back_send, back_recv = sems
+    chips = smp // 2
+    core, chip = lax.rem(mine_s, 2), mine_s // 2
+    sibling = mine_s + 1 - 2 * core
+    half = gram.shape[0] // 2
+    size = half // PARTS
+
+    def rows_of(owner, part):
+        return pl.ds(pl.multiple_of(owner * half + part * size, 8), size)
+
+    first = []
+    for part in range(PARTS):
+        copy = pltpu.make_async_remote_copy(
+            src_ref=gram.at[rows_of(1 - core, part)],
+            dst_ref=from_core.at[part],
+            send_sem=core_send.at[part],
+            recv_sem=core_recv.at[part],
+            device_id={"smp": sibling},
+            device_id_type=MESH,
+        )
+        copy.start()
+        first.append(copy)
+    second = []
+    for part in range(PARTS):
+        first[part].wait_recv()
+        over_chip[chip, part] = gram[rows_of(core, part), :] + from_core[part]
+        row = []
+        for distance in range(1, chips):
+            peer = lax.rem(chip + distance, chips)
+            copy = pltpu.make_async_remote_copy(
+                src_ref=over_chip.at[chip, part],
+                dst_ref=over_chip.at[chip, part],
+                send_sem=chip_send.at[distance, part],
+                recv_sem=chip_recv.at[distance, part],
+                device_id={"smp": peer * 2 + core},
+                device_id_type=MESH,
+            )
+            copy.start()
+            row.append(copy)
+        second.append(row)
+    return first, second, sibling, rows_of
+
+
+def finish_gram(full, over_chip, mine_s, smp, sems, first, second, sibling, rows_of):
+    back_send, back_recv = sems[4:]
+    core = lax.rem(mine_s, 2)
+    third = []
+    for part in range(PARTS):
+        for copy in second[part]:
+            copy.wait_recv()
+        total = over_chip[0, part]
+        for chip in range(1, smp // 2):
+            total = total + over_chip[chip, part]
+        full[rows_of(core, part), :] = total
+        copy = pltpu.make_async_remote_copy(
+            src_ref=full.at[rows_of(core, part)],
+            dst_ref=full.at[rows_of(core, part)],
+            send_sem=back_send.at[part],
+            recv_sem=back_recv.at[part],
+            device_id={"smp": sibling},
+            device_id_type=MESH,
+        )
+        copy.start()
+        third.append(copy)
+    for copy in third:
+        copy.wait_recv()
+    for copy in first + [copy for row in second for copy in row] + third:
+        copy.wait_send()
+
+
+def ridge_solve(full, square, width, total_samples):
+    cross = []
+    start = 0
+    for stop in range(TILE, width + 1, TILE):
+        column = slice(stop - TILE, stop)
+        for row in range(0, stop, TILE):
+            block = full[start + row : start + row + TILE, :]
+            for piece in range(3):
+                part = block.astype(jnp.bfloat16)
+                square[piece, row : row + TILE, column] = part
+                block = block - part.astype(jnp.float32)
+            if row + TILE < stop:
+                block = full[start + row : start + row + TILE, :].T
+                for piece in range(3):
+                    part = block.astype(jnp.bfloat16)
+                    square[piece, column, row : row + TILE] = part
+                    block = block - part.astype(jnp.float32)
+        cross.append(full[start + stop : start + stop + 1, :])
+        start += stop + 8
+    rank = lax.broadcasted_iota(jnp.int32, (8, 1), 0)
+    shifts = jnp.full((8, 1), penalty_list[-1] * total_samples, jnp.float32)
+    for index, penalty in enumerate(penalty_list):
+        shifts = jnp.where(rank == index, jnp.float32(penalty * total_samples), shifts)
+    residual = jnp.broadcast_to(jnp.concatenate(cross, axis=1), (8, width))
+    solution = jnp.zeros_like(residual)
+    direction = residual
+    norm_now = jnp.sum(residual * residual, axis=1, keepdims=True)
+    for ridge_step in range(RIDGE_STEPS):
+        middle = low_part(direction)
+        stacked = jnp.concatenate([direction, middle, low_part(middle)], axis=0)
+        stacked = stacked.astype(jnp.bfloat16)
+        product = jnp.dot(stacked, square[0], preferred_element_type=jnp.float32)
+        for piece in range(1, 3):
+            product = product + jnp.dot(
+                stacked, square[piece], preferred_element_type=jnp.float32
+            )
+        image = product[:8] + (product[8:16] + product[16:24]) + shifts * direction
+        alpha = norm_now / jnp.sum(direction * image, axis=1, keepdims=True)
+        solution = solution + alpha * direction
+        if ridge_step < RIDGE_STEPS - 1:
+            residual = residual - alpha * image
+            norm_next = jnp.sum(residual * residual, axis=1, keepdims=True)
+            direction = residual + (norm_next / norm_now) * direction
+            norm_now = norm_next
+    return solution.astype(jnp.bfloat16)
+
+
+def whole_kernel(
+    blk, smp, total_samples, cohort_count,
+    geno_ref, presence_ref, cohort_ref, fold_ref, pheno_ref, level_ref, linear_ref,
+    geno, pres, gram, from_core, over_chip, full, square, masked_ridge, scores_ref,
     gathered, packed, pieces, smp_part, blk_part,
+    load_sem, core_send, core_recv, chip_send, chip_recv, back_send, back_recv,
     score_send, score_recv, smp_send, smp_recv, blk_send, blk_recv,
 ):
     mine_b = lax.axis_index("blk")
@@ -97,6 +238,16 @@
     per_block = scores_ref.shape[0]
     owned = packed.shape[1]
     predictors = packed.shape[0]
+    local_count, width = geno.shape
+    chunks = load_sem.shape[0]
+    chunk = local_count // chunks
+
+    def load(index):
+        rows = pl.ds(pl.multiple_of(index * chunk, chunk), chunk)
+        return pltpu.make_async_copy(geno_ref.at[rows], geno.at[rows], load_sem.at[index])
+
+    for index in range(chunks):
+        load(index).start()
     barrier = pltpu.get_barrier_semaphore()
     for distance in range(1, blk):
         pl.semaphore_signal(
@@ -106,12 +257,24 @@
         pl.semaphore_signal(
             barrier, inc=1, device_id={"smp": lax.rem(mine_s + distance, smp)}, device_id_type=MESH
         )
+    pres[...] = jnp.zeros_like(pres)
+    pres[:cohort_count, :] = presence_ref[...].astype(jnp.float32)
+    accumulate_gram(chunk, chunks, load, geno, pres, cohort_ref, fold_ref, pheno_ref, gram)
     pl.semaphore_wait(barrier, blk + smp - 2)
 
-    copies = []
-    for distance in range(1, blk):
+    sems = (core_send, core_recv, chip_send, chip_recv, back_send, back_recv)
+    state = sum_gram(gram, from_core, over_chip, mine_s, smp, sems)
+    finish_gram(full, over_chip, mine_s, smp, sems, *state)
+    ridge = ridge_solve(full, square, width, total_samples).astype(jnp.float32)
+    for cohort in range(cohort_count):
+        masked_ridge[cohort * 8 : cohort * 8 + 8, :] = (
+            ridge * pres[cohort : cohort + 1, :]
+        ).astype(jnp.bfloat16)
+    scale = jnp.sqrt(jnp.float32(total_samples) / width)
+
+    def score_copy(distance):
         target = lax.rem(mine_b + distance, blk)
-        copy = pltpu.make_async_remote_copy(
+        return pltpu.make_async_remote_copy(
             src_ref=scores_ref.at[:, pl.ds(pl.multiple_of(target * owned, LANES), owned)],
             dst_ref=gathered.at[mine_b],
             send_sem=score_send.at[distance],
@@ -119,8 +282,28 @@
             device_id={"blk": target},
             device_id_type=MESH,
         )
-        copy.start()
-        copies.append(copy)
+
+    def score_chunk(distance):
+        target = lax.rem(mine_b + distance, blk)
+        rows = pl.ds(pl.multiple_of(target * owned, LANES), owned)
+        each = lax.dot_general(
+            masked_ridge[...], geno[rows, :], (((1,), (1,)), ((), ())),
+            preferred_element_type=jnp.float32,
+        )
+        cohort = cohort_ref[:, rows]
+        chosen = each[:8]
+        for index in range(1, cohort_count):
+            chosen = jnp.where(cohort == index, each[index * 8 : index * 8 + 8], chosen)
+        scores_ref[:, rows] = chosen[:per_block] * scale
+
+    def score_step(distance, _):
+        score_chunk(distance)
+        score_copy(distance).start()
+        return 0
+
+    lax.fori_loop(1, blk, score_step, 0)
+    score_chunk(0)
+    copies = [score_copy(distance) for distance in range(1, blk)]
     own = pl.ds(pl.multiple_of(mine_b * owned, LANES), owned)
     gathered[mine_b] = scores_ref[:, own]
     labels = pheno_ref[:, own].astype(jnp.float32)
@@ -181,67 +364,60 @@
     ]
 
 
-def level_one_fit(scores, fold_id, phenotype, total_samples):
+def on_device(genotype, presence, cohort_id, fold_id, phenotype):
     blk = lax.axis_size("blk")
     smp = lax.axis_size("smp")
-    per_block, local_count = scores.shape
+    local_count, block_width = genotype.shape
+    total_samples = local_count * smp
+    per_block = len(penalty_list)
     owned = local_count // blk
     predictors = per_block * blk
     width = predictors + 8
+    cohort_count = presence.shape[0]
+    half = gram_rows(block_width) // 2
+    size = half // PARTS
+    chips = smp // 2
     dma = pltpu.SemaphoreType.DMA
+    vmem = pl.BlockSpec(memory_space=pltpu.VMEM)
     level, linear = pl.pallas_call(
-        functools.partial(level_one_kernel, blk, smp, total_samples),
+        functools.partial(whole_kernel, blk, smp, total_samples, cohort_count),
         out_shape=(
             jax.ShapeDtypeStruct((1, predictors), jnp.float32),
             jax.ShapeDtypeStruct((1, owned), jnp.float32),
         ),
-        in_specs=[pl.BlockSpec(memory_space=pltpu.VMEM)] * 3,
-        out_specs=(pl.BlockSpec(memory_space=pltpu.VMEM),) * 2,
+        in_specs=[pl.BlockSpec(memory_space=pl.ANY)] + [vmem] * 4,
+        out_specs=(vmem,) * 2,
         scratch_shapes=[
+            pltpu.VMEM((local_count, block_width), jnp.bfloat16),
+            pltpu.VMEM((8, block_width), jnp.float32),
+            pltpu.VMEM((2 * half, TILE), jnp.float32),
+            pltpu.VMEM((PARTS, size, TILE), jnp.float32),
+            pltpu.VMEM((chips, PARTS, size, TILE), jnp.float32),
+            pltpu.VMEM((2 * half, TILE), jnp.float32),
+            pltpu.VMEM((3, block_width, block_width), jnp.bfloat16),
+            pltpu.VMEM((8 * cohort_count, block_width), jnp.bfloat16),
+            pltpu.VMEM((per_block, local_count), jnp.float32),
             pltpu.VMEM((blk, per_block, owned), jnp.float32),
             pltpu.VMEM((predictors, owned), jnp.float32),
             pltpu.VMEM((2 * predictors, owned), jnp.bfloat16),
             pltpu.VMEM((NEWTON, smp, predictors, width), jnp.float32),
             pltpu.VMEM((NEWTON, blk, predictors, width), jnp.float32),
+            dma((local_count // CHUNK,)),
+            dma((PARTS,)), dma((PARTS,)),
+            dma((chips, PARTS)), dma((chips, PARTS)),
+            dma((PARTS,)), dma((PARTS,)),
             dma((blk,)), dma((blk,)),
             dma((NEWTON, smp)), dma((NEWTON, smp)),
             dma((NEWTON, blk)), dma((NEWTON, blk)),
         ],
         compiler_params=pltpu.CompilerParams(
-            collective_id=0, has_side_effects=True, vmem_limit_bytes=48 * 1024 * 1024
+            collective_id=0, has_side_effects=True, vmem_limit_bytes=56 * 1024 * 1024
         ),
-    )(scores, fold_id.reshape(1, -1), phenotype.reshape(1, -1))
+    )(
+        genotype, presence, cohort_id.reshape(1, -1), fold_id.reshape(1, -1),
+        phenotype.reshape(1, -1),
+    )
     return level.reshape(predictors), linear.reshape(owned)
-
-
-def on_device(genotype, presence, cohort_id, fold_id, phenotype):
-    local_count = genotype.shape[0]
-    width = genotype.shape[1]
-    total_samples = local_count * lax.axis_size("smp")
-    train = (fold_id != 0).astype(jnp.float32)
-    target = 2.0 * phenotype.astype(jnp.float32) - 1.0
-    onehot = (cohort_id[:, None] == jnp.arange(presence.shape[0], dtype=jnp.int32)[None, :]).astype(
-        jnp.bfloat16
-    )
-    present_rows = jnp.dot(
-        onehot, presence.astype(jnp.bfloat16), preferred_element_type=jnp.float32
-    ).astype(jnp.bfloat16)
-    masked = genotype * present_rows
-    weighted = masked * train.astype(jnp.bfloat16)[:, None]
-    gram = lax.dot_general(
-        weighted, masked, (((0,), (0,)), ((), ())), preferred_element_type=jnp.float32
-    )
-    cross = jnp.dot(
-        (train * target).astype(jnp.bfloat16), masked, preferred_element_type=jnp.float32
-    )
-    gram, cross = lax.psum((gram, cross), "smp")
-    shifts = jnp.array([penalty * total_samples for penalty in penalty_list], jnp.float32)
-    ridge = ridge_solve(gram, cross, shifts, RIDGE_STEPS).astype(jnp.bfloat16)
-    scores = lax.dot_general(
-        ridge, masked, (((1,), (1,)), ((), ())), preferred_element_type=jnp.float32
-    )
-    scores = scores * jnp.sqrt(jnp.float32(total_samples) / width)
-    return level_one_fit(scores, fold_id, phenotype, total_samples)
 
 
 def solution(mesh):

time: 141 us -> 84.4 us (0.60)
  matrix products: 33.6 us -> 0 us
  Pallas kernels: 50.3 us -> 81.1 us
  waiting for transfers between devices: 25.3 us -> 0 us
  between operations: 14.1 us -> 0.64 us
  blocking collectives: 8.68 us -> 0 us
  other arithmetic: 3.93 us -> 0 us
  local copies, waits for them, and re-layouts: 4.35 us -> 2.4 us
    dot_general x10 -> x0, matrix products: 33.6 us -> none  [the longest x6 11.7 us: ridge_solve(): jnp.dot(direction, gram, precision=high) + shifts[:, None] * direction]
    pallas_call x1, Pallas kernels: 50.3 us -> 81.1 us  [on_device(): pl.pallas_call(functools.partial(whole_kernel, blk, smp, total_samples, c...]
    psum x1 -> x0, waiting for transfers between devices: 25.3 us -> none  [on_device(): gram, cross = lax.psum((gram, cross), 'smp')]
    psum x1 -> x0, blocking collectives: 8.68 us -> none  [on_device(): gram, cross = lax.psum((gram, cross), 'smp')]
    unnamed x10 -> x2, local copies, waits for them, and re-layouts: 4.33 us -> 2.4 us
    reduce_sum x6 -> x0, other arithmetic: 1.55 us -> none  [the longest x5 0.95 us: ridge_solve(): norm_next = jnp.sum(residual * residual, axis=1)]
  transfers between devices with their start and end apart: 1 -> 0, of which waited for: 1 -> 0; matrix products, arithmetic and copies ran while one was open for 4% -> 0% of each run, Pallas kernels for 0% -> 0%
where the time goes in v2:
time: 84.4 us; the launch traced here: 84.1 us
  Pallas kernels  81.1 us (96%)
  local copies, waits for them, and re-layouts  2.4 us (3%)
    pallas_call x1, Pallas kernels, on_device(): pl.pallas_call(functools.partial(whole_kernel, blk, smp, total_samples, c...  81.1 us
    unnamed x2, local copies, waits for them, and re-layouts  2.4 us

profile of v2, /device:TPU:0, one launch (start us, length us, event | category | flops | bytes accessed | tf_op | source)
XLA Modules:
  0.0 84.1 jit_solution(11700476747194363635)
XLA Ops:
  0.6 81.1 %shard_map.68 = (f32[1,40]{1,0:T(1,128)}, f32[1,1024]{1,0:T(1,128)}) custom-call(bf16[8192,512]{1,0:T(8,128)(2,1)} %geno_ref.1, s32[6,512]{1,0:T(8,128)} %presence_ref.1, s32[1,8192]{1,0:T(1,128)} %bitcast.5, s32[1,8192]{1,0:T(1,128)} %bitcast.6, s32[1,8192]{1,0:T(1,128)} %bitcast.7), custom_call_target="tpu_custom_call" | custom-call | tf_op jit(solution)/shard_map/pallas_call | solution.py:382
  81.7 1.1 %copy.9 = f32[40]{0:T(128)} copy(f32[40]{0:T(128)} %bitcast.9) | data formatting | bytes 320
  82.9 1.3 %copy.10 = f32[1024]{0:T(1024)} copy(f32[1024]{0:T(1024)} %bitcast.8) | data formatting | bytes 8192

commit v3 on v2

--- a/solution.py
+++ b/solution.py
@@ -13,7 +13,7 @@
 LANES = 128
 TILE = 256
 PARTS = 7
-CHUNK = 1024
+CHUNK = 2048
 MESH = pl.DeviceIdType.MESH
 
 
@@ -47,6 +47,35 @@
                 entry = other[j : j + 1, :] * inverse
                 columns[k - start] = jnp.where(row_of_lane == j, entry, other - column * entry)
     return jnp.broadcast_to(system[:, order : order + 1], (order, LANES))
+
+
+def pack_plan(predictors):
+    lanes = -(-(predictors + 1) // 2) * 2
+    groups = max(1, LANES // lanes)
+    rows = -(-predictors // (8 * groups)) * 8
+    return lanes, groups, rows, -(-lanes * groups // LANES) * LANES
+
+
+def pack_rows(system):
+    lanes, groups, rows, width = pack_plan(system.shape[0])
+    out = system[:rows]
+    for group in range(1, groups):
+        block = system[group * rows : (group + 1) * rows]
+        if block.shape[0] < rows:
+            block = jnp.concatenate(
+                [block, jnp.zeros((rows - block.shape[0], width), jnp.float32)], axis=0
+            )
+        out = out + pltpu.roll(block, group * lanes, 1)
+    return out
+
+
+def unpack_rows(packed_rows, predictors):
+    lanes, groups, rows, width = pack_plan(predictors)
+    blocks = [packed_rows]
+    for group in range(1, groups):
+        block = pltpu.roll(packed_rows, width - group * lanes, 1)
+        blocks.append(block[: min(rows, predictors - group * rows)])
+    return jnp.concatenate(blocks, axis=0)
 
 
 def exchange(ref, mine, axis, count, send_sem, recv_sem):
@@ -317,8 +346,8 @@
     for copy in copies:
         copy.wait_send()
 
-    width = predictors + 8
-    pad_row = lax.broadcasted_iota(jnp.int32, (8, owned), 0)
+    width = pack_plan(predictors)[3]
+    pad_row = lax.broadcasted_iota(jnp.int32, (width - predictors, owned), 0)
     row_of = lax.broadcasted_iota(jnp.int32, (predictors, width), 0)
     column_of = lax.broadcasted_iota(jnp.int32, (predictors, width), 1)
     ridge = level_ridge * total_samples
@@ -344,7 +373,7 @@
                 pieces[...], part.astype(jnp.bfloat16), (((1,), (1,)), ((), ())),
                 preferred_element_type=jnp.float32,
             )
-        smp_part[step, mine_s] = moments[:predictors] + moments[predictors:]
+        smp_part[step, mine_s] = pack_rows(moments[:predictors] + moments[predictors:])
         over_smp = exchange(
             smp_part.at[step], mine_s, "smp", smp, smp_send.at[step], smp_recv.at[step]
         )
@@ -352,6 +381,7 @@
         system = exchange(
             blk_part.at[step], mine_b, "blk", blk, blk_send.at[step], blk_recv.at[step]
         )
+        system = unpack_rows(system, predictors)
         system = jnp.where(row_of == column_of, system + ridge, system)
         system = jnp.where(column_of == predictors, system - ridge * widen(level), system)
         return level + spd_solve(system, predictors)
@@ -372,7 +402,7 @@
     per_block = len(penalty_list)
     owned = local_count // blk
     predictors = per_block * blk
-    width = predictors + 8
+    system_rows, system_lanes = pack_plan(predictors)[2:]
     cohort_count = presence.shape[0]
     half = gram_rows(block_width) // 2
     size = half // PARTS
@@ -400,8 +430,8 @@
             pltpu.VMEM((blk, per_block, owned), jnp.float32),
             pltpu.VMEM((predictors, owned), jnp.float32),
             pltpu.VMEM((2 * predictors, owned), jnp.bfloat16),
-            pltpu.VMEM((NEWTON, smp, predictors, width), jnp.float32),
-            pltpu.VMEM((NEWTON, blk, predictors, width), jnp.float32),
+            pltpu.VMEM((NEWTON, smp, system_rows, system_lanes), jnp.float32),
+            pltpu.VMEM((NEWTON, blk, system_rows, system_lanes), jnp.float32),
             dma((local_count // CHUNK,)),
             dma((PARTS,)), dma((PARTS,)),
             dma((chips, PARTS)), dma((chips, PARTS)),

time: 84.4 us -> 77.6 us (0.919)
  Pallas kernels: 81.1 us -> 74.3 us
    pallas_call x1, Pallas kernels: 81.1 us -> 74.3 us  [on_device(): pl.pallas_call(functools.partial(whole_kernel, blk, smp, total_samples, c...]
where the time goes in v3:
time: 77.6 us; the launch traced here: 77.4 us
  Pallas kernels  74.3 us (96%)
  local copies, waits for them, and re-layouts  2.4 us (3%)
    pallas_call x1, Pallas kernels, on_device(): pl.pallas_call(functools.partial(whole_kernel, blk, smp, total_samples, c...  74.3 us
    unnamed x2, local copies, waits for them, and re-layouts  2.4 us

profile of v3, /device:TPU:0, one launch (start us, length us, event | category | flops | bytes accessed | tf_op | source)
XLA Modules:
  0.0 77.4 jit_solution(9976711707927808927)
XLA Ops:
  0.6 74.3 %shard_map.68 = (f32[1,40]{1,0:T(1,128)}, f32[1,1024]{1,0:T(1,128)}) custom-call(bf16[8192,512]{1,0:T(8,128)(2,1)} %geno_ref.1, s32[6,512]{1,0:T(8,128)} %presence_ref.1, s32[1,8192]{1,0:T(1,128)} %bitcast.5, s32[1,8192]{1,0:T(1,128)} %bitcast.6, s32[1,8192]{1,0:T(1,128)} %bitcast.7), custom_call_target="tpu_custom_call" | custom-call | tf_op jit(solution)/shard_map/pallas_call | solution.py:412
  75.0 1.1 %copy.9 = f32[40]{0:T(128)} copy(f32[40]{0:T(128)} %bitcast.9) | data formatting | bytes 320
  76.1 1.3 %copy.10 = f32[1024]{0:T(1024)} copy(f32[1024]{0:T(1024)} %bitcast.8) | data formatting | bytes 8192

commit v4 on v3

--- a/solution.py
+++ b/solution.py
@@ -214,13 +214,13 @@
         column = slice(stop - TILE, stop)
         for row in range(0, stop, TILE):
             block = full[start + row : start + row + TILE, :]
-            for piece in range(3):
+            for piece in range(2):
                 part = block.astype(jnp.bfloat16)
                 square[piece, row : row + TILE, column] = part
                 block = block - part.astype(jnp.float32)
             if row + TILE < stop:
                 block = full[start + row : start + row + TILE, :].T
-                for piece in range(3):
+                for piece in range(2):
                     part = block.astype(jnp.bfloat16)
                     square[piece, column, row : row + TILE] = part
                     block = block - part.astype(jnp.float32)
@@ -239,7 +239,7 @@
         stacked = jnp.concatenate([direction, middle, low_part(middle)], axis=0)
         stacked = stacked.astype(jnp.bfloat16)
         product = jnp.dot(stacked, square[0], preferred_element_type=jnp.float32)
-        for piece in range(1, 3):
+        for piece in range(1, 2):
             product = product + jnp.dot(
                 stacked, square[piece], preferred_element_type=jnp.float32
             )
@@ -424,7 +424,7 @@
             pltpu.VMEM((PARTS, size, TILE), jnp.float32),
             pltpu.VMEM((chips, PARTS, size, TILE), jnp.float32),
             pltpu.VMEM((2 * half, TILE), jnp.float32),
-            pltpu.VMEM((3, block_width, block_width), jnp.bfloat16),
+            pltpu.VMEM((2, block_width, block_width), jnp.bfloat16),
             pltpu.VMEM((8 * cohort_count, block_width), jnp.bfloat16),
             pltpu.VMEM((per_block, local_count), jnp.float32),
             pltpu.VMEM((blk, per_block, owned), jnp.float32),

time: 77.6 us -> 77.1 us (level)
  no operation moved by 1% of the time
where the time goes in v4:
time: 77.1 us; the launch traced here: 76.8 us
  Pallas kernels  73.8 us (96%)
  local copies, waits for them, and re-layouts  2.4 us (3%)
    pallas_call x1, Pallas kernels, on_device(): pl.pallas_call(functools.partial(whole_kernel, blk, smp, total_samples, c...  73.8 us
    unnamed x2, local copies, waits for them, and re-layouts  2.4 us

profile of v4, /device:TPU:0, one launch (start us, length us, event | category | flops | bytes accessed | tf_op | source)
XLA Modules:
  0.0 76.8 jit_solution(5659972308632611666)
XLA Ops:
  0.6 73.8 %shard_map.68 = (f32[1,40]{1,0:T(1,128)}, f32[1,1024]{1,0:T(1,128)}) custom-call(bf16[8192,512]{1,0:T(8,128)(2,1)} %geno_ref.1, s32[6,512]{1,0:T(8,128)} %presence_ref.1, s32[1,8192]{1,0:T(1,128)} %bitcast.5, s32[1,8192]{1,0:T(1,128)} %bitcast.6, s32[1,8192]{1,0:T(1,128)} %bitcast.7), custom_call_target="tpu_custom_call" | custom-call | tf_op jit(solution)/shard_map/pallas_call | solution.py:412
  74.4 1.1 %copy.9 = f32[40]{0:T(128)} copy(f32[40]{0:T(128)} %bitcast.9) | data formatting | bytes 320
  75.6 1.3 %copy.10 = f32[1024]{0:T(1024)} copy(f32[1024]{0:T(1024)} %bitcast.8) | data formatting | bytes 8192
